TPU v7x, 32 devices: a whole 2x2x4 slice. The times are simulated.
32 devices in a mesh: groups: 2 (over y), wide: 4 (over x, core), narrow: 4 (over z).
Axes of the slice: x: 2, y: 2, z: 4, core: 2. Of those that a mesh axis runs over, the one named last changes fastest.
Arguments:
- activations: bfloat16 [8192, 28672], P(('groups', 'narrow'), 'wide'), parts along dimension 0, may hold values from -6 to 6
- out_grads: bfloat16 [8192, 8192], P(('groups', 'wide'), 'narrow'), parts along dimension 0, may hold values from -6 to 6
- basis_in: bfloat16 [28672, 512], P('wide', 'narrow'), may hold values from -0.03125 to 0.03125
- basis_out: bfloat16 [8192, 512], P('narrow', 'wide'), may hold values from -0.0625 to 0.0625
Outputs:
- correction: float32 [1024, 512], P(('groups', 'wide'), 'narrow'), parts along dimension 0
There are 2 independent parts, one for each index of `groups`. A program takes and returns all parts, laid end to end along the dimension named above; an argument that names none is the same for every part. Nothing has to cross between parts.
All inputs are finite; a program needn't handle non-finite values.
Results may differ from a plain program's by a relative error of at most 0.0027.
Values may be sent and summed in bfloat16 or wider, within the bound.
A program may use at most 192 MiB of HBM per device.

v0:
```python
import functools

import jax
import jax.numpy as jnp
from jax import lax
from jax.experimental import pallas as pl
from jax.experimental.pallas import tpu as pltpu
from jax.sharding import PartitionSpec as P

LEN = 512
SEQS = 8
CHUNKS = 4
OUT_STEP = 5
MESH = pl.DeviceIdType.MESH


def fit_kernel(
    W, N,
    act, og, bi, bo, out,
    act_v, og_v, bi_v, bo_v, pin, rsbuf, proj_in, out_send, out_recv, out_t, sq, sq_recv,
    local_sem, z_send, z_recv, y_send, y_recv, bo_send, bo_recv,
    rs_send, rs_recv, ag_send, ag_recv, po_send, po_recv, sq_send, sq_rsem,
):
    g, w, z = lax.axis_index("groups"), lax.axis_index("wide"), lax.axis_index("narrow")
    T, F = act.shape
    K = bi.shape[1]
    C = CHUNKS
    half = F // 2
    rows_c = half // C
    Q = T // W
    steps = (N - 1) * C

    def remote(src, dst, send, recv, dev):
        return pltpu.make_async_remote_copy(
            src_ref=src, dst_ref=dst, send_sem=send, recv_sem=recv, device_id=dev, device_id_type=MESH
        )

    barrier = pltpu.get_barrier_semaphore()
    for k in range(1, W):
        pl.semaphore_signal(barrier, inc=1, device_id=(g, lax.rem(w + k, W), z), device_id_type=MESH)
    for k in range(1, N):
        pl.semaphore_signal(barrier, inc=1, device_id=(g, w, lax.rem(z + k, N)), device_id_type=MESH)
    pl.semaphore_signal(barrier, inc=1, device_id=(1 - g, w, z), device_id_type=MESH)
    for k in range(N):
        @pl.when(jnp.logical_or(w != z, z != k))
        def _():
            pl.semaphore_signal(barrier, inc=1, device_id=(g, z, k), device_id_type=MESH)

    copies = [
        pltpu.make_async_copy(bi, bi_v.at[z], local_sem.at[0]),
        pltpu.make_async_copy(act, act_v, local_sem.at[1]),
        pltpu.make_async_copy(bo, bo_v.at[w], local_sem.at[2]),
        pltpu.make_async_copy(og, og_v, local_sem.at[3]),
    ]
    for copy in copies:
        copy.start()
    pl.semaphore_wait(barrier, W - 1 + N - 1 + 1 + N - jnp.where(w == z, 1, 0))

    def rows_of(h, c):
        return pl.ds(pl.multiple_of(h * half + c * rows_c, 128), rows_c)

    sides = ((0, 1), (1, -1))

    def exists(at):
        return jnp.logical_and(at >= 0, at < N)

    def own_send(side, sgn, c):
        r = rows_of(g, c)
        return remote(bi.at[r], bi_v.at[z, r], z_send.at[side, c], z_recv.at[side, c], (g, w, z + sgn))

    def chunk(side, sgn, t):
        return z - sgn * (t // C + 1), lax.rem(t, C)

    def z_copy(side, sgn, t):
        b, c = chunk(side, sgn, t)
        r = rows_of(g, c)
        return remote(
            bi_v.at[b, r], bi_v.at[b, r], z_send.at[side, t + C], z_recv.at[side, t + C], (g, w, z + sgn)
        )

    def z_arrival(side, sgn, t):
        b, c = chunk(side, sgn, t)
        r = rows_of(g, c)
        return remote(
            bi_v.at[b, r], bi_v.at[b, r], z_send.at[side, t], z_recv.at[side, t], (g, w, z - sgn)
        )

    def y_copy(side, sgn, t, h):
        b, c = chunk(side, sgn, t)
        r = rows_of(h, c)
        return remote(
            bi_v.at[b, r], bi_v.at[b, r], y_send.at[side, t], y_recv.at[side, t], (1 - g, w, z)
        )

    for c in range(C):
        for side, sgn in sides:
            @pl.when(exists(z + sgn))
            def _():
                own_send(side, sgn, c).start()

    def bo_copy(k):
        return remote(
            bo, bo_v.at[w], bo_send.at[k - 1], bo_recv.at[k - 1], (g, lax.rem(w + k, W), z)
        )

    def bo_arrival(k):
        return remote(
            bo, bo_v.at[lax.rem(w + W - k, W)], bo_send.at[k - 1], bo_recv.at[k - 1],
            (g, lax.rem(w + W - k, W), z),
        )

    for k in range(1, W):
        bo_copy(k).start()

    pin[...] = jnp.zeros_like(pin)

    def accumulate(b, h, c):
        r = rows_of(h, c)
        pin[b] += jnp.dot(act_v[:, r], bi_v[b, r, :], preferred_element_type=jnp.float32)

    def quarter(at):
        return pl.ds(pl.multiple_of(at * Q, 16), Q)

    def rs_copy(b, k):
        to = lax.rem(w + k, W)
        return remote(
            pin.at[b, quarter(to)], rsbuf.at[b, k - 1], rs_send.at[b, k - 1], rs_recv.at[b, k - 1], (g, to, z)
        )

    def ag_copy(b, k):
        to = lax.rem(w + k, W)
        q = quarter(w)
        return remote(
            proj_in.at[b, q], proj_in.at[b, q], ag_send.at[b, k - 1], ag_recv.at[b, k - 1], (g, to, z)
        )

    def ag_arrival(b, k):
        origin = lax.rem(w + W - k, W)
        q = quarter(origin)
        return remote(
            proj_in.at[b, q], proj_in.at[b, q], ag_send.at[b, k - 1], ag_recv.at[b, k - 1], (g, origin, z)
        )

    def start_sum(b):
        for k in range(1, W):
            rs_copy(b, k).start()

    def finish_sum(b):
        total = pin[b, quarter(w), :]
        for k in range(1, W):
            rs_copy(b, k).wait_recv()
            total += rsbuf[b, k - 1]
        proj_in[b, quarter(w), :] = total.astype(proj_in.dtype)
        for k in range(1, W):
            ag_copy(b, k).start()

    def po_copy(to):
        return remote(
            out_send.at[to], out_recv.at[z], po_send.at[to], po_recv.at[z], (g, to, w)
        )

    def po_arrival(k):
        return remote(
            out_send.at[w], out_recv.at[k], po_send.at[w], po_recv.at[k], (g, z, k)
        )

    copies[0].wait()
    copies[1].wait()

    def own_step(i, carry):
        accumulate(z, i // C, lax.rem(i, C))
        return carry

    lax.fori_loop(0, 2 * C, own_step, 0)

    def step(t, carry):
        for side, sgn in sides:
            arriving = C * (z if sgn == 1 else N - 1 - z)

            @pl.when(t < arriving)
            def _():
                z_arrival(side, sgn, t).wait_recv()

                @pl.when(exists(z + sgn))
                def _():
                    z_copy(side, sgn, t).start()

                y_copy(side, sgn, t, g).start()
        for side, sgn in sides:
            arriving = C * (z if sgn == 1 else N - 1 - z)

            @pl.when(t < arriving)
            def _():
                b, c = chunk(side, sgn, t)
                accumulate(b, g, c)

            @pl.when(jnp.logical_and(t >= 1, t - 1 < arriving))
            def _():
                b, c = chunk(side, sgn, t - 1)
                y_copy(side, sgn, t - 1, 1 - g).wait_recv()
                accumulate(b, 1 - g, c)

                @pl.when(c == C - 1)
                def _():
                    start_sum(b)

        @pl.when(t == 0)
        def _():
            start_sum(z)

        @pl.when(t == 2)
        def _():
            finish_sum(z)

        for side, sgn in sides:
            d = (t - 2) // C
            b = z - sgn * d

            @pl.when(jnp.logical_and(jnp.logical_and(t > 2, lax.rem(t, C) == 2 % C), exists(b)))
            def _():
                finish_sum(b)

        @pl.when(t == OUT_STEP)
        def _():
            copies[2].wait()
            copies[3].wait()
            for k in range(1, W):
                bo_arrival(k).wait_recv()

        @pl.when(jnp.logical_and(t >= OUT_STEP, t < OUT_STEP + W))
        def _():
            to = t - OUT_STEP
            part = jnp.dot(og_v[...], bo_v[to], preferred_element_type=jnp.float32)
            local = jnp.logical_and(to == w, w == z)
            part = part.astype(out_send.dtype)

            @pl.when(local)
            def _():
                out_recv[z] = part

            @pl.when(jnp.logical_not(local))
            def _():
                out_send[to] = part
                po_copy(to).start()

        return carry

    lax.fori_loop(0, steps + 1, step, 0)

    for k in range(N):
        @pl.when(jnp.logical_or(w != z, z != k))
        def _():
            po_arrival(k).wait_recv()
    total = out_recv[0].astype(jnp.float32)
    for k in range(1, N):
        total += out_recv[k].astype(jnp.float32)
    out_t[...] = total.T.astype(out_t.dtype)

    def sq_copy(b):
        return remote(sq.at[b], sq_recv.at[z], sq_send.at[b], sq_rsem.at[z], (g, w, b))

    def sq_arrival(k):
        return remote(sq.at[k], sq_recv.at[k], sq_send.at[k], sq_rsem.at[k], (g, w, k))

    def squares(b):
        for k in range(1, W):
            ag_arrival(b, k).wait_recv()
        total = jnp.zeros((K, K), jnp.float32)
        for s in range(T // LEN):
            span = slice(s * LEN, (s + 1) * LEN)
            pgrad = jnp.dot(out_t[:, span], proj_in[b, span, :], preferred_element_type=jnp.float32)
            total += pgrad * pgrad
        sq[b] = total

    squares(z)
    for d in range(1, N):
        for side, sgn in sides:
            b = z - sgn * d

            @pl.when(exists(b))
            def _():
                if d == N - 1:
                    finish_sum(b)
                squares(b)
                sq_copy(b).start()

    total = sq[z]
    for k in range(1, N):
        origin = lax.rem(z + k, N)
        sq_arrival(origin).wait_recv()
        total += sq_recv[origin]
    out[...] = total / (SEQS * LEN)

    for side, sgn in sides:
        arriving = C * (z if sgn == 1 else N - 1 - z)

        @pl.when(exists(z + sgn))
        def _():
            for c in range(C):
                own_send(side, sgn, c).wait_send()

        def drain(t, carry):
            @pl.when(t < arriving)
            def _():
                @pl.when(exists(z + sgn))
                def _():
                    z_copy(side, sgn, t).wait_send()

                y_copy(side, sgn, t, g).wait_send()
            return carry

        lax.fori_loop(0, steps, drain, 0)
    for k in range(1, W):
        bo_copy(k).wait_send()
        for b in range(N):
            rs_copy(b, k).wait_send()
            ag_copy(b, k).wait_send()
    for to in range(W):
        @pl.when(jnp.logical_or(w != z, to != w))
        def _():
            po_copy(to).wait_send()
    for k in range(1, N):
        sq_copy(lax.rem(z + k, N)).wait_send()


def one_kernel(W, N, act, og, bi, bo):
    T, F = act.shape
    D = og.shape[1]
    K = bi.shape[1]
    bf, f32 = jnp.bfloat16, jnp.float32
    dma = pltpu.SemaphoreType.DMA
    steps = (N - 1) * CHUNKS
    return pl.pallas_call(
        functools.partial(fit_kernel, W, N),
        out_shape=jax.ShapeDtypeStruct((K, K), f32),
        in_specs=[pl.BlockSpec(memory_space=pl.ANY)] * 4,
        out_specs=pl.BlockSpec(memory_space=pltpu.VMEM),
        scratch_shapes=[
            pltpu.VMEM((T, F), bf),
            pltpu.VMEM((T, D), bf),
            pltpu.VMEM((N, F, K), bf),
            pltpu.VMEM((W, D, K), bf),
            pltpu.VMEM((N, T, K), f32),
            pltpu.VMEM((N, W - 1, T // W, K), f32),
            pltpu.VMEM((N, T, K), bf),
            pltpu.VMEM((W, T, K), bf),
            pltpu.VMEM((N, T, K), bf),
            pltpu.VMEM((K, T), bf),
            pltpu.VMEM((N, K, K), f32),
            pltpu.VMEM((N, K, K), f32),
            dma((4,)),
            dma((2, steps + CHUNKS)),
            dma((2, steps + CHUNKS)),
            dma((2, steps)),
            dma((2, steps)),
            dma((W - 1,)),
            dma((W - 1,)),
            dma((N, W - 1)),
            dma((N, W - 1)),
            dma((N, W - 1)),
            dma((N, W - 1)),
            dma((W,)),
            dma((N,)),
            dma((N,)),
            dma((N,)),
        ],
        compiler_params=pltpu.CompilerParams(
            collective_id=0, has_side_effects=True, vmem_limit_bytes=52 * 2**20
        ),
        cost_estimate=pl.CostEstimate(
            flops=2 * T * (F * N * K + D * W * K), bytes_accessed=2 * T * (F + D), transcendentals=0
        ),
    )(act, og, bi, bo)


def projections_everywhere(activations, out_grads, basis_in, basis_out):
    partial_in = jnp.dot(
        lax.all_gather(activations, "narrow", axis=0, tiled=True),
        basis_in,
        preferred_element_type=jnp.float32,
    )
    proj_in = lax.psum(partial_in, "wide").astype(jnp.bfloat16)
    partial_out = jnp.dot(
        lax.all_gather(out_grads, "wide", axis=0, tiled=True),
        basis_out,
        preferred_element_type=jnp.float32,
    )
    proj_out = lax.psum(partial_out, "narrow").astype(jnp.bfloat16)
    seq_in = proj_in.reshape(SEQS, LEN, proj_in.shape[1])
    seq_out = proj_out.reshape(SEQS, LEN, proj_out.shape[1])
    pgrad = jnp.einsum("slg,sla->sga", seq_out, seq_in, preferred_element_type=jnp.float32)
    return jnp.sum(pgrad * pgrad, axis=0) / (SEQS * LEN)


def solution(mesh):
    in_specs = (
        P(("groups", "narrow"), "wide"),
        P(("groups", "wide"), "narrow"),
        P("wide", "narrow"),
        P("narrow", "wide"),
    )
    out_specs = P(("groups", "wide"), "narrow")
    W, N = mesh.shape["wide"], mesh.shape["narrow"]
    on_device = projections_everywhere
    if mesh.shape["groups"] == 2 and W == N and SEQS % N == 0:
        on_device = functools.partial(one_kernel, W, N)
    return jax.shard_map(
        on_device, mesh=mesh, in_specs=in_specs, out_specs=out_specs, check_vma=False
    )
```

profile of v0, /device:TPU:0, one launch (start us, length us, event | category | flops | bytes accessed | tf_op | source)
XLA Modules:
  0.0 118.1 jit_solution(8722755647820035460)
XLA Ops:
  0.0 0.0 copy-start
  0.0 1.0 copy-done
  1.0 116.4 %shard_map.46 = f32[128,128]{1,0:T(8,128)S(1)} custom-call(bf16[1024,7168]{1,0:T(8,128)(2,1)} %act.1, bf16[1024,2048]{1,0:T(8,128)(2,1)} %og.1, bf16[7168,128]{1,0:T(8,128)(2,1)} %bi.1, bf16[2048,128]{1,0:T(8,128)(2,1)S(1)} %copy-done), custom_call_target="tpu_custom_call" | custom-call | flops 9663676416 | bytes 18874368 | tf_op jit(solution)/shard_map/pallas_call | solution.py:333
  117.5 0.6 copy.6
Async XLA Ops:
  0.0 1.0 copy-start
where the time goes:
time: 118 us
  Pallas kernels  116 us (98%)
  local copies, waits for them, and re-layouts  1.67 us (1%)
    pallas_call x1, Pallas kernels, one_kernel(): pl.pallas_call(functools.partial(fit_kernel, W, N), out_shape=jax.ShapeDt...  116 us

commit v1 on v0

--- a/solution.py
+++ b/solution.py
@@ -29,6 +29,8 @@
     rows_c = half // C
     Q = T // W
     steps = (N - 1) * C
+    farthest = jnp.maximum(z, N - 1 - z)
+    lag = jnp.where(farthest == N - 1, 1, C)
 
     def remote(src, dst, send, recv, dev):
         return pltpu.make_async_remote_copy(
@@ -194,10 +196,10 @@
                 b, c = chunk(side, sgn, t)
                 accumulate(b, g, c)
 
-            @pl.when(jnp.logical_and(t >= 1, t - 1 < arriving))
-            def _():
-                b, c = chunk(side, sgn, t - 1)
-                y_copy(side, sgn, t - 1, 1 - g).wait_recv()
+            @pl.when(jnp.logical_and(t >= lag, t - lag < arriving))
+            def _():
+                b, c = chunk(side, sgn, t - lag)
+                y_copy(side, sgn, t - lag, 1 - g).wait_recv()
                 accumulate(b, 1 - g, c)
 
                 @pl.when(c == C - 1)
@@ -213,10 +215,12 @@
             finish_sum(z)
 
         for side, sgn in sides:
-            d = (t - 2) // C
+            since = t - 1 - lag
+            d = lax.max(since, 0) // C
             b = z - sgn * d
-
-            @pl.when(jnp.logical_and(jnp.logical_and(t > 2, lax.rem(t, C) == 2 % C), exists(b)))
+            due = jnp.logical_and(since == d * C, jnp.logical_and(d > 0, d < farthest))
+
+            @pl.when(jnp.logical_and(due, exists(b)))
             def _():
                 finish_sum(b)
 
@@ -279,8 +283,10 @@
 
             @pl.when(exists(b))
             def _():
-                if d == N - 1:
+                @pl.when(farthest == d)
+                def _():
                     finish_sum(b)
+
                 squares(b)
                 sq_copy(b).start()
 

time: 118 us -> 116 us (0.983)
  Pallas kernels: 116 us -> 114 us
    pallas_call x1, Pallas kernels: 116 us -> 114 us  [one_kernel(): pl.pallas_call(functools.partial(fit_kernel, W, N), out_shape=jax.ShapeDt...]
where the time goes in v1:
time: 116 us
  Pallas kernels  114 us (98%)
  local copies, waits for them, and re-layouts  1.67 us (1%)
    pallas_call x1, Pallas kernels, one_kernel(): pl.pallas_call(functools.partial(fit_kernel, W, N), out_shape=jax.ShapeDt...  114 us

profile of v1, /device:TPU:0, one launch (start us, length us, event | category | flops | bytes accessed | tf_op | source)
XLA Modules:
  0.0 115.5 jit_solution(8741790511194737941)
XLA Ops:
  0.0 0.0 copy-start
  0.0 1.0 copy-done
  1.0 113.9 %shard_map.46 = f32[128,128]{1,0:T(8,128)S(1)} custom-call(bf16[1024,7168]{1,0:T(8,128)(2,1)} %act.1, bf16[1024,2048]{1,0:T(8,128)(2,1)} %og.1, bf16[7168,128]{1,0:T(8,128)(2,1)} %bi.1, bf16[2048,128]{1,0:T(8,128)(2,1)S(1)} %copy-done), custom_call_target="tpu_custom_call" | custom-call | flops 9663676416 | bytes 18874368 | tf_op jit(solution)/shard_map/pallas_call | solution.py:339
  114.9 0.6 copy.6
Async XLA Ops:
  0.0 1.0 copy-start

commit v2 on v1

--- a/solution.py
+++ b/solution.py
@@ -233,7 +233,7 @@
 
         @pl.when(jnp.logical_and(t >= OUT_STEP, t < OUT_STEP + W))
         def _():
-            to = t - OUT_STEP
+            to = lax.rem(w + z + t - OUT_STEP, W)
             part = jnp.dot(og_v[...], bo_v[to], preferred_element_type=jnp.float32)
             local = jnp.logical_and(to == w, w == z)
             part = part.astype(out_send.dtype)

time: 116 us -> 117 us (level)
  no operation moved by 1% of the time
where the time goes in v2:
time: 117 us; the launch traced here: 116 us
  Pallas kernels  114 us (97%)
  local copies, waits for them, and re-layouts  1.67 us (1%)
    pallas_call x1, Pallas kernels, one_kernel(): pl.pallas_call(functools.partial(fit_kernel, W, N), out_shape=jax.ShapeDt...  114 us

profile of v2, /device:TPU:0, one launch (start us, length us, event | category | flops | bytes accessed | tf_op | source)
XLA Modules:
  0.0 115.6 jit_solution(7701776153438886188)
XLA Ops:
  0.0 0.0 copy-start
  0.0 1.0 copy-done
  1.0 113.9 %shard_map.46 = f32[128,128]{1,0:T(8,128)S(1)} custom-call(bf16[1024,7168]{1,0:T(8,128)(2,1)} %act.1, bf16[1024,2048]{1,0:T(8,128)(2,1)} %og.1, bf16[7168,128]{1,0:T(8,128)(2,1)} %bi.1, bf16[2048,128]{1,0:T(8,128)(2,1)S(1)} %copy-done), custom_call_target="tpu_custom_call" | custom-call | flops 9663676416 | bytes 18874368 | tf_op jit(solution)/shard_map/pallas_call | solution.py:339
  115.0 0.6 copy.6
Async XLA Ops:
  0.0 1.0 copy-start
